TPU v7x, 32 devices: a whole 2x2x4 slice. The times are simulated.
32 devices in a mesh: row: 8 (over z, core), col: 4 (over y, x).
Axes of the slice: x: 2, y: 2, z: 4, core: 2. Of those that a mesh axis runs over, the one named last changes fastest.
Arguments:
- a_blocks: bfloat16 [8, 4, 32, 128, 128], P('row', 'col'), may hold values from -6 to 6
- a_coord: int32 [8, 4, 32, 2], P('row', 'col'), may hold values from -1 to 31, as said below
- b_blocks: bfloat16 [8, 4, 32, 128, 128], P('row', 'col'), may hold values from -0.125 to 0.125
- b_coord: int32 [8, 4, 32, 2], P('row', 'col'), may hold values from -1 to 31, as said below
- c_mask: int32 [32, 32], P('row', 'col'), may hold values 0 or 1
Outputs:
- c_blocks: float32 [4096, 4096], P('row', 'col')
Inputs may be any that keep to these rules, and one draw needn't show every extreme that they name: `a_coord`: entry [i, s, t] holds the block row and block column of the block in slot t of device (i, s), or -1 in both for an empty slot. Its block row lies in i * 4 to (i + 1) * 4 - 1. With p = column // 4, slot t lies in t // 8 = (p - i) mod 4. No block is named twice. `b_coord`: entry [s, j, t] holds the block row and block column of the block in slot t of device (s, j), or -1 in both for an empty slot. Its block column lies in j * 8 to (j + 1) * 8 - 1. With p = row // 4, slot t lies in t // 4 = (p - j) mod 8. No block is named twice.
All inputs are finite; a program needn't handle non-finite values. No bound on the sum of `c_mask` on one device may be relied on, other than what follows from the above.
Results may differ from a plain program's by a relative error of at most 0.0003.
Values may be sent and summed in bfloat16 or wider, within the bound.
A program may use at most 64 MiB of HBM per device.

v0:
```python
import jax
import jax.numpy as jnp
from jax import lax
from jax.sharding import PartitionSpec as P


def passed_along(value, axis, steps):
    count = lax.axis_size(axis)
    pairs = [(source, (source + steps) % count) for source in range(count)]
    return lax.ppermute(value, axis, pairs)


def roll_panel(panel_b):
    return passed_along(panel_b, "row", -1)


def shards(a_blocks, a_coord, b_blocks, b_coord, c_mask):
    row_count = lax.axis_size("row")
    col_count = lax.axis_size("col")
    panel_ratio = row_count // col_count
    grid_row = lax.axis_index("row")
    grid_col = lax.axis_index("col")
    block_size = a_blocks.shape[-1]
    band_rows = c_mask.shape[0]
    band_cols = c_mask.shape[1]
    a_send = a_blocks.reshape(col_count, -1, block_size, block_size)
    a_tags = a_coord.reshape(col_count, -1, 2)
    a_recv, a_tags = (
        lax.all_to_all(a_send, "col", split_axis=0, concat_axis=0, tiled=True),
        lax.all_to_all(a_tags, "col", split_axis=0, concat_axis=0, tiled=True),
    )
    a_recv = a_recv.reshape(-1, block_size, block_size)
    a_tags = a_tags.reshape(-1, 2)
    a_live = a_tags[:, 0] >= 0
    panel_index = a_tags[:, 1] // band_rows
    count_a = panel_ratio * band_rows * band_rows
    a_pos = (
        panel_index // col_count * band_rows * band_rows
        + (a_tags[:, 0] - grid_row * band_rows) * band_rows
        + a_tags[:, 1] % band_rows
    )
    a_pos = jnp.where(a_live, a_pos, count_a)
    a_tile = (
        jnp.zeros((count_a, block_size, block_size), a_blocks.dtype)
        .at[a_pos]
        .set(a_recv, mode="drop")
    )
    a_group = a_tile.reshape(panel_ratio, band_rows, band_rows, block_size, block_size)
    a_group = a_group.transpose(0, 1, 3, 2, 4).reshape(
        panel_ratio, band_rows * block_size, band_rows * block_size
    )
    b_send = b_blocks.reshape(row_count, -1, block_size, block_size)
    b_tags = b_coord.reshape(row_count, -1, 2)
    b_recv, b_tags = (
        lax.all_to_all(b_send, "row", split_axis=0, concat_axis=0, tiled=True),
        lax.all_to_all(b_tags, "row", split_axis=0, concat_axis=0, tiled=True),
    )
    b_recv = b_recv.reshape(-1, block_size, block_size)
    b_tags = b_tags.reshape(-1, 2)
    b_live = b_tags[:, 0] >= 0
    count_b = band_rows * band_cols
    b_pos = b_tags[:, 0] % band_rows * band_cols + b_tags[:, 1] - grid_col * band_cols
    b_pos = jnp.where(b_live, b_pos, count_b)
    b_tile = (
        jnp.zeros((count_b, block_size, block_size), b_blocks.dtype)
        .at[b_pos]
        .set(b_recv, mode="drop")
    )
    b_panel = b_tile.reshape(band_rows, band_cols, block_size, block_size)
    b_panel = b_panel.transpose(0, 2, 1, 3).reshape(band_rows * block_size, band_cols * block_size)
    offset = grid_row + grid_col
    accumulated = jnp.zeros((band_rows * block_size, band_cols * block_size), jnp.float32)

    def advance(step_index, carried):
        a_current, panel_b, running = carried
        member = (offset + step_index) % row_count // col_count
        a_use = lax.dynamic_index_in_dim(a_current, member, 0, keepdims=False)
        running = running + jnp.dot(a_use, panel_b, preferred_element_type=jnp.float32)
        a_current = passed_along(a_current, "col", -1)
        return (a_current, roll_panel(panel_b), running)

    a_last, b_last, accumulated = lax.fori_loop(
        0, row_count - 1, advance, (a_group, b_panel, accumulated)
    )
    member = (offset + row_count - 1) % row_count // col_count
    a_use = lax.dynamic_index_in_dim(a_last, member, 0, keepdims=False)
    accumulated = accumulated + jnp.dot(a_use, b_last, preferred_element_type=jnp.float32)
    masked = accumulated.reshape(band_rows, block_size, band_cols, block_size) * c_mask[
        :, None, :, None
    ].astype(jnp.float32)
    return masked.reshape(band_rows * block_size, band_cols * block_size)


def solution(mesh):
    placed = (
        P("row", "col", None, None, None),
        P("row", "col", None, None),
        P("row", "col", None, None, None),
        P("row", "col", None, None),
        P("row", "col"),
    )
    return jax.shard_map(
        shards, mesh=mesh, in_specs=placed, out_specs=P("row", "col"), check_vma=False
    )
```

profile of v0, /device:TPU:0, one launch (start us, length us, event | category | flops | bytes accessed | tf_op | source)
XLA Modules:
  0.0 258.3 jit_solution(16308488505931294219)
XLA Ops:
  1.4 5.2 %all-to-all-start = ((s32[4,8,2]{1,2,0:T(2,128)}), s32[4,8,2]{1,2,0:T(2,128)S(1)}, u32[]{:S(2)}, u32[]{:S(2)}) async-start(s32[4,8,2]{1,2,0:T(2,128)} %copy.8), calls=%async_computation | async-start | bytes 8192 | tf_op jit(solution)/shard_map/all_to_all | solution.py:30
  7.3 3.9 %all-to-all-done = s32[4,8,2]{1,2,0:T(2,128)S(1)} async-done(((s32[4,8,2]{1,2,0:T(2,128)}), s32[4,8,2]{1,2,0:T(2,128)S(1)}, u32[]{:S(2)}, u32[]{:S(2)}) %all-to-all-start) | async-done | bytes 288 | tf_op jit(solution)/shard_map/all_to_all | solution.py:30
  11.2 10.3 %all_to_all.20 = s32[8,4,2]{1,2,0:T(2,128)S(1)} all-to-all(s32[8,4,2]{1,2,0:T(2,128)S(1)} %copy.11), channel_id=1, replica_groups=mesh['row'=8,'col'=4] {'row'}, dimensions={0} | all-to-all | bytes 512 | tf_op jit(solution)/shard_map/all_to_all | solution.py:56
  21.5 18.8 %all_to_all.21 = bf16[4,8,128,128]{3,2,1,0:T(8,128)(2,1)} all-to-all(bf16[4,8,128,128]{3,2,1,0:T(8,128)(2,1)} %bitcast.48), channel_id=1, replica_groups=mesh['row'=8,'col'=4] {'col'}, dimensions={0} | all-to-all | bytes 2097152 | tf_op jit(solution)/shard_map/all_to_all | solution.py:29
  40.3 4.2 %all-to-all-start.3 = ((bf16[8,4,128,128]{3,2,1,0:T(8,128)(2,1)}), bf16[8,4,128,128]{3,2,1,0:T(8,128)(2,1)}, u32[]{:S(2)}, u32[]{:S(2)}) async-start(bf16[8,4,128,128]{3,2,1,0:T(8,128)(2,1)} %bitcast.6), calls=%async_computation.3 | async-start | bytes 2097152 | tf_op jit(solution)/shard_map/all_to_all | solution.py:55
  45.1 3.6 %scatter_fusion = bf16[32,128,128]{2,1,0:T(8,128)(2,1)S(1)} fusion(bf16[32,128,128]{2,1,0:T(8,128)(2,1)S(1)} %broadcast.69.clone, s32[32]{0:T(128)S(1)} %fusion.9, bf16[32,128,128]{2,1,0:T(8,128)(2,1)} %bitcast.46), kind=kCustom, calls=%fused_computation | custom fusion | bytes 3145856 | tf_op jit(solution)/shard_map/scatter | solution.py:46
  48.7 1.8 copy.10
  50.5 2.2 reshape.46
  52.7 18.4 %all-to-all-done.3 = bf16[8,4,128,128]{3,2,1,0:T(8,128)(2,1)} async-done(((bf16[8,4,128,128]{3,2,1,0:T(8,128)(2,1)}), bf16[8,4,128,128]{3,2,1,0:T(8,128)(2,1)}, u32[]{:S(2)}, u32[]{:S(2)}) %all-to-all-start.3) | async-done | bytes 1048608 | tf_op jit(solution)/shard_map/all_to_all | solution.py:55
  71.4 3.6 %scatter_fusion.1 = bf16[32,128,128]{2,1,0:T(8,128)(2,1)S(1)} fusion(bf16[32,128,128]{2,1,0:T(8,128)(2,1)S(1)} %broadcast.69.clone.1, s32[32]{0:T(128)S(1)} %fusion.10, bf16[32,128,128]{2,1,0:T(8,128)(2,1)} %bitcast.7), kind=kCustom, calls=%fused_computation.1 | custom fusion | bytes 3145856 | tf_op jit(solution)/shard_map/scatter | solution.py:67
  75.7 1.3 copy.18
  76.9 177.6 %while.20 = (s32[]{:T(128)}, bf16[2,512,512]{2,1,0:T(8,128)(2,1)}, bf16[512,1024]{1,0:T(8,128)(2,1)}, f32[512,1024]{1,0:T(8,128)S(1)}, s32[]{:T(128)}, /*index=5...) while((s32[]{:T(128)}, bf16[2,512,512]{2,1,0:T(8,128)(2,1)}, ...), condition=%wide.region_3.4_spmd.clone, body=%wide.region_2.3_spmd.clone.sunk | while | flops 537919488 | bytes 18350596 | solution.py:82
  76.9 2.3 copy.26
  79.2 0.9 collective-permute-start
  80.1 1.2 copy.27
  82.0 2.1 select_add_fusion.2
  84.0 20.2 %collective-permute-done = bf16[2,512,512]{2,1,0:T(8,128)(2,1)} collective-permute-done((bf16[2,512,512]{2,1,0:T(8,128)(2,1)}, bf16[2,512,512]{2,1,0:T(8,128)(2,1)}, u32[]{:S(2)}, u32[]{:S(2)}) %collective-permute-start) | collective-permute-done | bytes 1048608 | tf_op jit(solution)/shard_map/while/body/eval_jaxpr/ppermute | solution.py:10
  104.2 2.3 copy.26
  106.5 1.8 collective-permute-start
  108.3 1.2 copy.27
  109.7 2.1 select_add_fusion.2
  111.8 18.9 %collective-permute-done = bf16[2,512,512]{2,1,0:T(8,128)(2,1)} collective-permute-done((bf16[2,512,512]{2,1,0:T(8,128)(2,1)}, bf16[2,512,512]{2,1,0:T(8,128)(2,1)}, u32[]{:S(2)}, u32[]{:S(2)}) %collective-permute-start) | collective-permute-done | bytes 1048608 | tf_op jit(solution)/shard_map/while/body/eval_jaxpr/ppermute | solution.py:10
  130.7 2.3 copy.26
  132.9 2.6 %collective-permute-start = (bf16[2,512,512]{2,1,0:T(8,128)(2,1)}, bf16[2,512,512]{2,1,0:T(8,128)(2,1)}, u32[]{:S(2)}, u32[]{:S(2)}) collective-permute-start(bf16[2,512,512]{2,1,0:T(8,128)(2,1)} %copy.26), channel_id=1, source_target_pairs={{0,3},{1,0},{2,1},{3,2},{4,7},{5,4},{6,5},{7,6},{8,11},{9,8},{10,9... | collective-permute-start | bytes 3145736 | tf_op jit(solution)/shard_map/while/body/eval_jaxpr/ppermute | solution.py:10
  135.5 1.2 copy.27
  136.8 2.1 select_add_fusion.2
  138.8 18.2 %collective-permute-done = bf16[2,512,512]{2,1,0:T(8,128)(2,1)} collective-permute-done((bf16[2,512,512]{2,1,0:T(8,128)(2,1)}, bf16[2,512,512]{2,1,0:T(8,128)(2,1)}, u32[]{:S(2)}, u32[]{:S(2)}) %collective-permute-start) | collective-permute-done | bytes 1048608 | tf_op jit(solution)/shard_map/while/body/eval_jaxpr/ppermute | solution.py:10
  157.0 2.3 copy.26
  159.3 2.6 %collective-permute-start = (bf16[2,512,512]{2,1,0:T(8,128)(2,1)}, bf16[2,512,512]{2,1,0:T(8,128)(2,1)}, u32[]{:S(2)}, u32[]{:S(2)}) collective-permute-start(bf16[2,512,512]{2,1,0:T(8,128)(2,1)} %copy.26), channel_id=1, source_target_pairs={{0,3},{1,0},{2,1},{3,2},{4,7},{5,4},{6,5},{7,6},{8,11},{9,8},{10,9... | collective-permute-start | bytes 3145736 | tf_op jit(solution)/shard_map/while/body/eval_jaxpr/ppermute | solution.py:10
  161.9 1.2 copy.27
  163.1 2.1 select_add_fusion.2
  165.2 17.3 %collective-permute-done = bf16[2,512,512]{2,1,0:T(8,128)(2,1)} collective-permute-done((bf16[2,512,512]{2,1,0:T(8,128)(2,1)}, bf16[2,512,512]{2,1,0:T(8,128)(2,1)}, u32[]{:S(2)}, u32[]{:S(2)}) %collective-permute-start) | collective-permute-done | bytes 1048608 | tf_op jit(solution)/shard_map/while/body/eval_jaxpr/ppermute | solution.py:10
  182.5 2.3 copy.26
  184.7 2.6 collective-permute-start
  187.3 1.2 copy.27
  188.5 2.1 select_add_fusion.2
  190.6 16.4 %collective-permute-done = bf16[2,512,512]{2,1,0:T(8,128)(2,1)} collective-permute-done((bf16[2,512,512]{2,1,0:T(8,128)(2,1)}, bf16[2,512,512]{2,1,0:T(8,128)(2,1)}, u32[]{:S(2)}, u32[]{:S(2)}) %collective-permute-start) | collective-permute-done | bytes 1048608 | tf_op jit(solution)/shard_map/while/body/eval_jaxpr/ppermute | solution.py:10
  207.0 2.3 copy.26
  209.2 2.5 collective-permute-start
  211.8 1.2 copy.27
  213.0 2.1 select_add_fusion.2
  215.1 15.5 %collective-permute-done = bf16[2,512,512]{2,1,0:T(8,128)(2,1)} collective-permute-done((bf16[2,512,512]{2,1,0:T(8,128)(2,1)}, bf16[2,512,512]{2,1,0:T(8,128)(2,1)}, u32[]{:S(2)}, u32[]{:S(2)}) %collective-permute-start) | collective-permute-done | bytes 1048608 | tf_op jit(solution)/shard_map/while/body/eval_jaxpr/ppermute | solution.py:10
  230.6 2.3 copy.26
  232.8 2.5 collective-permute-start
  235.3 1.2 copy.27
  236.6 2.1 select_add_fusion.2
  238.6 15.9 %collective-permute-done = bf16[2,512,512]{2,1,0:T(8,128)(2,1)} collective-permute-done((bf16[2,512,512]{2,1,0:T(8,128)(2,1)}, bf16[2,512,512]{2,1,0:T(8,128)(2,1)}, u32[]{:S(2)}, u32[]{:S(2)}) %collective-permute-start) | collective-permute-done | bytes 1048608 | tf_op jit(solution)/shard_map/while/body/eval_jaxpr/ppermute | solution.py:10
  254.7 3.6 %bitcast_multiply_fusion = f32[512,1024]{1,0:T(8,128)} fusion(f32[64,8,8,128]{3,2,1,0:T(8,128)S(1)} %bitcast.45, f32[512,1024]{1,0:T(8,128)S(1)} %get-tuple-element.142, bf16[512,1024]{1,0:T(8,128)(2,1)} %get-tuple-element.144, bf16[2,512,512]{2,1,0:T(8,128)(2,1)} %get-tuple-element.143, s32[]{:T(128)S(6)} %select_n.101), kind=kOutput, calls=%fused_computation.6 | convolution fusion | flops 537919488 | bytes 7864324 | tf_op jit(solution)/shard_map/dot_general | solution.py:87
  (32 shorter events, 4.6 us)
Async XLA Ops:
  1.4 9.8 %all-to-all-start = ((s32[4,8,2]{1,2,0:T(2,128)}), s32[4,8,2]{1,2,0:T(2,128)S(1)}, u32[]{:S(2)}, u32[]{:S(2)}) async-start(s32[4,8,2]{1,2,0:T(2,128)} %copy.8), calls=%async_computation | async-start | bytes 8192 | tf_op jit(solution)/shard_map/all_to_all | solution.py:30
  21.5 23.1 %copy-start = (s32[4,8]{1,0:T(4,128)S(1)}, s32[4,8]{1,0:T(4,128)}, u32[]{:S(2)}) copy-start(s32[4,8]{1,0:T(4,128)} %param.11) | copy-start | bytes 388
  40.3 30.8 %all-to-all-start.3 = ((bf16[8,4,128,128]{3,2,1,0:T(8,128)(2,1)}), bf16[8,4,128,128]{3,2,1,0:T(8,128)(2,1)}, u32[]{:S(2)}, u32[]{:S(2)}) async-start(bf16[8,4,128,128]{3,2,1,0:T(8,128)(2,1)} %bitcast.6), calls=%async_computation.3 | async-start | bytes 2097152 | tf_op jit(solution)/shard_map/all_to_all | solution.py:55
  79.2 25.0 %collective-permute-start = (bf16[2,512,512]{2,1,0:T(8,128)(2,1)}, bf16[2,512,512]{2,1,0:T(8,128)(2,1)}, u32[]{:S(2)}, u32[]{:S(2)}) collective-permute-start(bf16[2,512,512]{2,1,0:T(8,128)(2,1)} %copy.26), channel_id=1, source_target_pairs={{0,3},{1,0},{2,1},{3,2},{4,7},{5,4},{6,5},{7,6},{8,11},{9,8},{10,9... | collective-permute-start | bytes 3145736 | tf_op jit(solution)/shard_map/while/body/eval_jaxpr/ppermute | solution.py:10
  81.3 22.9 %collective-permute-start.1 = (bf16[512,1024]{1,0:T(8,128)(2,1)S(1)}, bf16[512,1024]{1,0:T(8,128)(2,1)}, u32[]{:S(2)}, u32[]{:S(2)}) collective-permute-start(bf16[512,1024]{1,0:T(8,128)(2,1)S(1)} %copy.27), channel_id=1, source_target_pairs={{0,28},{4,0},{8,4},{12,8},{16,12},{20,16},{24,20},{28,24},{1,29},{... | collective-permute-start | bytes 3145736 | tf_op jit(solution)/shard_map/while/body/eval_jaxpr/ppermute | solution.py:10
  106.5 24.2 %collective-permute-start = (bf16[2,512,512]{2,1,0:T(8,128)(2,1)}, bf16[2,512,512]{2,1,0:T(8,128)(2,1)}, u32[]{:S(2)}, u32[]{:S(2)}) collective-permute-start(bf16[2,512,512]{2,1,0:T(8,128)(2,1)} %copy.26), channel_id=1, source_target_pairs={{0,3},{1,0},{2,1},{3,2},{4,7},{5,4},{6,5},{7,6},{8,11},{9,8},{10,9... | collective-permute-start | bytes 3145736 | tf_op jit(solution)/shard_map/while/body/eval_jaxpr/ppermute | solution.py:10
  109.5 21.2 %collective-permute-start.1 = (bf16[512,1024]{1,0:T(8,128)(2,1)S(1)}, bf16[512,1024]{1,0:T(8,128)(2,1)}, u32[]{:S(2)}, u32[]{:S(2)}) collective-permute-start(bf16[512,1024]{1,0:T(8,128)(2,1)S(1)} %copy.27), channel_id=1, source_target_pairs={{0,28},{4,0},{8,4},{12,8},{16,12},{20,16},{24,20},{28,24},{1,29},{... | collective-permute-start | bytes 3145736 | tf_op jit(solution)/shard_map/while/body/eval_jaxpr/ppermute | solution.py:10
  132.9 24.1 %collective-permute-start = (bf16[2,512,512]{2,1,0:T(8,128)(2,1)}, bf16[2,512,512]{2,1,0:T(8,128)(2,1)}, u32[]{:S(2)}, u32[]{:S(2)}) collective-permute-start(bf16[2,512,512]{2,1,0:T(8,128)(2,1)} %copy.26), channel_id=1, source_target_pairs={{0,3},{1,0},{2,1},{3,2},{4,7},{5,4},{6,5},{7,6},{8,11},{9,8},{10,9... | collective-permute-start | bytes 3145736 | tf_op jit(solution)/shard_map/while/body/eval_jaxpr/ppermute | solution.py:10
  136.8 20.3 %collective-permute-start.1 = (bf16[512,1024]{1,0:T(8,128)(2,1)S(1)}, bf16[512,1024]{1,0:T(8,128)(2,1)}, u32[]{:S(2)}, u32[]{:S(2)}) collective-permute-start(bf16[512,1024]{1,0:T(8,128)(2,1)S(1)} %copy.27), channel_id=1, source_target_pairs={{0,28},{4,0},{8,4},{12,8},{16,12},{20,16},{24,20},{28,24},{1,29},{... | collective-permute-start | bytes 3145736 | tf_op jit(solution)/shard_map/while/body/eval_jaxpr/ppermute | solution.py:10
  159.3 23.2 %collective-permute-start = (bf16[2,512,512]{2,1,0:T(8,128)(2,1)}, bf16[2,512,512]{2,1,0:T(8,128)(2,1)}, u32[]{:S(2)}, u32[]{:S(2)}) collective-permute-start(bf16[2,512,512]{2,1,0:T(8,128)(2,1)} %copy.26), channel_id=1, source_target_pairs={{0,3},{1,0},{2,1},{3,2},{4,7},{5,4},{6,5},{7,6},{8,11},{9,8},{10,9... | collective-permute-start | bytes 3145736 | tf_op jit(solution)/shard_map/while/body/eval_jaxpr/ppermute | solution.py:10
  163.1 19.4 %collective-permute-start.1 = (bf16[512,1024]{1,0:T(8,128)(2,1)S(1)}, bf16[512,1024]{1,0:T(8,128)(2,1)}, u32[]{:S(2)}, u32[]{:S(2)}) collective-permute-start(bf16[512,1024]{1,0:T(8,128)(2,1)S(1)} %copy.27), channel_id=1, source_target_pairs={{0,28},{4,0},{8,4},{12,8},{16,12},{20,16},{24,20},{28,24},{1,29},{... | collective-permute-start | bytes 3145736 | tf_op jit(solution)/shard_map/while/body/eval_jaxpr/ppermute | solution.py:10
  184.7 22.2 %collective-permute-start = (bf16[2,512,512]{2,1,0:T(8,128)(2,1)}, bf16[2,512,512]{2,1,0:T(8,128)(2,1)}, u32[]{:S(2)}, u32[]{:S(2)}) collective-permute-start(bf16[2,512,512]{2,1,0:T(8,128)(2,1)} %copy.26), channel_id=1, source_target_pairs={{0,3},{1,0},{2,1},{3,2},{4,7},{5,4},{6,5},{7,6},{8,11},{9,8},{10,9... | collective-permute-start | bytes 3145736 | tf_op jit(solution)/shard_map/while/body/eval_jaxpr/ppermute | solution.py:10
  188.5 18.5 %collective-permute-start.1 = (bf16[512,1024]{1,0:T(8,128)(2,1)S(1)}, bf16[512,1024]{1,0:T(8,128)(2,1)}, u32[]{:S(2)}, u32[]{:S(2)}) collective-permute-start(bf16[512,1024]{1,0:T(8,128)(2,1)S(1)} %copy.27), channel_id=1, source_target_pairs={{0,28},{4,0},{8,4},{12,8},{16,12},{20,16},{24,20},{28,24},{1,29},{... | collective-permute-start | bytes 3145736 | tf_op jit(solution)/shard_map/while/body/eval_jaxpr/ppermute | solution.py:10
  209.2 21.3 %collective-permute-start = (bf16[2,512,512]{2,1,0:T(8,128)(2,1)}, bf16[2,512,512]{2,1,0:T(8,128)(2,1)}, u32[]{:S(2)}, u32[]{:S(2)}) collective-permute-start(bf16[2,512,512]{2,1,0:T(8,128)(2,1)} %copy.26), channel_id=1, source_target_pairs={{0,3},{1,0},{2,1},{3,2},{4,7},{5,4},{6,5},{7,6},{8,11},{9,8},{10,9... | collective-permute-start | bytes 3145736 | tf_op jit(solution)/shard_map/while/body/eval_jaxpr/ppermute | solution.py:10
  213.0 17.6 %collective-permute-start.1 = (bf16[512,1024]{1,0:T(8,128)(2,1)S(1)}, bf16[512,1024]{1,0:T(8,128)(2,1)}, u32[]{:S(2)}, u32[]{:S(2)}) collective-permute-start(bf16[512,1024]{1,0:T(8,128)(2,1)S(1)} %copy.27), channel_id=1, source_target_pairs={{0,28},{4,0},{8,4},{12,8},{16,12},{20,16},{24,20},{28,24},{1,29},{... | collective-permute-start | bytes 3145736 | tf_op jit(solution)/shard_map/while/body/eval_jaxpr/ppermute | solution.py:10
  232.8 21.7 %collective-permute-start = (bf16[2,512,512]{2,1,0:T(8,128)(2,1)}, bf16[2,512,512]{2,1,0:T(8,128)(2,1)}, u32[]{:S(2)}, u32[]{:S(2)}) collective-permute-start(bf16[2,512,512]{2,1,0:T(8,128)(2,1)} %copy.26), channel_id=1, source_target_pairs={{0,3},{1,0},{2,1},{3,2},{4,7},{5,4},{6,5},{7,6},{8,11},{9,8},{10,9... | collective-permute-start | bytes 3145736 | tf_op jit(solution)/shard_map/while/body/eval_jaxpr/ppermute | solution.py:10
  236.6 18.0 %collective-permute-start.1 = (bf16[512,1024]{1,0:T(8,128)(2,1)S(1)}, bf16[512,1024]{1,0:T(8,128)(2,1)}, u32[]{:S(2)}, u32[]{:S(2)}) collective-permute-start(bf16[512,1024]{1,0:T(8,128)(2,1)S(1)} %copy.27), channel_id=1, source_target_pairs={{0,28},{4,0},{8,4},{12,8},{16,12},{20,16},{24,20},{28,24},{1,29},{... | collective-permute-start | bytes 3145736 | tf_op jit(solution)/shard_map/while/body/eval_jaxpr/ppermute | solution.py:10
where the time goes:
time: 260 us; the launch traced here: 258 us
  waiting for transfers between devices  145 us (56%)
  local copies, waits for them, and re-layouts  40.5 us (16%)
  blocking collectives  29.1 us (11%)
  starting transfers between devices  25.8 us (10%)
  matrix products  18 us (7%)
    ppermute x14, waiting for transfers between devices, passed_along(): return lax.ppermute(value, axis, pairs)  122 us
    while x14, local copies, waits for them, and re-layouts  24.4 us
    all_to_all x1, blocking collectives, shards(): lax.all_to_all(a_send, 'col', split_axis=0, concat_axis=0, tiled=True)  18.8 us
    all_to_all x1, waiting for transfers between devices, shards(): lax.all_to_all(b_send, 'row', split_axis=0, concat_axis=0, tiled=True)  18.4 us
    ppermute x14, starting transfers between devices, passed_along(): return lax.ppermute(value, axis, pairs)  16.4 us
    dot_general x7, matrix products, advance(): jnp.dot(a_use, panel_b, preferred_element_type=jnp.float32)  14.4 us
    all_to_all x1, blocking collectives, shards(): lax.all_to_all(b_tags, 'row', split_axis=0, concat_axis=0, tiled=True)  10.3 us
  transfers between devices with their start and end apart: 16, of which 9 were waited for; matrix products, arithmetic and copies ran while one was open for 12% of the time, Pallas kernels for 0%

commit v1 on v0

v1 whole, which is shorter than its diff:
```python
import functools

import jax
import jax.numpy as jnp
from jax import lax
from jax.experimental import pallas as pl
from jax.experimental.pallas import tpu as pltpu
from jax.sharding import PartitionSpec as P

MESH = pl.DeviceIdType.MESH
AHEAD = 3


def kernel(
    rows, cols, slots, band_rows, band_cols,
    a_ref, b_ref, code_a_ref, code_b_ref, o_ref, *scratch,
):
    panels = rows
    chips = rows // 2
    cap_a, cap_b = slots // cols, slots // rows
    ratio = panels // cols
    nb = panels * band_rows
    bs = a_ref.shape[-1]
    buf_a = scratch[:cols]
    buf_b = scratch[cols : cols + panels]
    (
        tile_a, tile_b, codes_a, codes_b, inv_v, inv_s,
        own_a_sem, own_b_sem, a_send, a_recv, ca_send, ca_recv, cb_send, cb_recv,
        up_send, down_send, z_recv, sib_send, sib_recv, local_sem,
    ) = scratch[cols + panels :]

    r = lax.axis_index("row")
    c = lax.axis_index("col")
    z = r // 2
    core = r % 2
    sibling = z * 2 + (1 - core)

    barrier = pltpu.get_barrier_semaphore()
    for off in range(1, cols):
        pl.semaphore_signal(barrier, inc=1, device_id=(r, (c + off) % cols), device_id_type=MESH)
    for off in range(1, rows):
        pl.semaphore_signal(barrier, inc=1, device_id=((r + off) % rows, c), device_id_type=MESH)

    order = [s + m * cols for s in range(cols) for m in range(ratio)]

    def own_a(s):
        group = (s - r % cols + cols) % cols
        return pltpu.make_async_copy(
            a_ref.at[pl.ds(group * cap_a, cap_a)],
            buf_a[s].at[pl.ds(1 + c * cap_a, cap_a)], own_a_sem.at[s])

    def send_a(s, off):
        group = (s - r % cols + cols) % cols
        return pltpu.make_async_remote_copy(
            src_ref=a_ref.at[pl.ds(group * cap_a, cap_a)],
            dst_ref=buf_a[s].at[pl.ds(1 + c * cap_a, cap_a)],
            send_sem=a_send.at[s, off - 1], recv_sem=a_recv.at[s, off - 1],
            device_id=(r, (c + off) % cols), device_id_type=MESH)

    def take_a(s, off):
        source = (c - off + cols) % cols
        return pltpu.make_async_remote_copy(
            src_ref=a_ref.at[pl.ds(0, cap_a)],
            dst_ref=buf_a[s].at[pl.ds(1 + source * cap_a, cap_a)],
            send_sem=a_send.at[s, off - 1], recv_sem=a_recv.at[s, off - 1],
            device_id=(r, (c + off) % cols), device_id_type=MESH)

    def own_slots(p):
        group = (p - c + panels) % panels
        return b_ref.at[pl.ds(group * cap_b, cap_b)]

    def place(p, owner_row):
        return buf_b[p].at[pl.ds(1 + owner_row * cap_b, cap_b)]

    def own_b(p):
        return pltpu.make_async_copy(own_slots(p), place(p, r), own_b_sem.at[p])

    def along(p, chip, up, own):
        owner = chip * 2 + core
        step = 2 if up else -2
        return pltpu.make_async_remote_copy(
            src_ref=own_slots(p) if own else place(p, owner), dst_ref=place(p, owner),
            send_sem=(up_send if up else down_send).at[p, chip], recv_sem=z_recv.at[p, chip],
            device_id=(r + step, c), device_id_type=MESH)

    def across(p, chip, own):
        owner = chip * 2 + core
        return pltpu.make_async_remote_copy(
            src_ref=own_slots(p) if own else place(p, owner), dst_ref=place(p, owner),
            send_sem=sib_send.at[p, chip], recv_sem=sib_recv.at[p, chip],
            device_id=(sibling, c), device_id_type=MESH)

    def take_across(p, chip):
        owner = chip * 2 + (1 - core)
        return pltpu.make_async_remote_copy(
            src_ref=place(p, owner), dst_ref=place(p, owner),
            send_sem=sib_send.at[p, chip], recv_sem=sib_recv.at[p, chip],
            device_id=(sibling, c), device_id_type=MESH)

    def code_a(off, source):
        return pltpu.make_async_remote_copy(
            src_ref=code_a_ref, dst_ref=codes_a.at[pl.ds(source * slots, slots)],
            send_sem=ca_send.at[off - 1], recv_sem=ca_recv.at[off - 1],
            device_id=(r, (c + off) % cols), device_id_type=MESH)

    def code_b(off, source):
        return pltpu.make_async_remote_copy(
            src_ref=code_b_ref, dst_ref=codes_b.at[pl.ds(source * slots, slots)],
            send_sem=cb_send.at[off - 1], recv_sem=cb_recv.at[off - 1],
            device_id=((r + off) % rows, c), device_id_type=MESH)

    def start_own_b(p):
        @pl.when(z > 0)
        def _():
            along(p, z, False, True).start()

        @pl.when(z < chips - 1)
        def _():
            along(p, z, True, True).start()

        across(p, z, True).start()

    def start_a(s):
        for off in range(1, cols):
            send_a(s, off).start()

    pl.semaphore_wait(barrier, rows + cols - 2)
    start_own_b(order[0])
    start_a(0)
    for off in range(1, cols):
        code_a(off, c).start()
    for off in range(1, rows):
        code_b(off, r).start()
    for k in range(1, min(AHEAD, panels)):
        start_own_b(order[k])
    if cols > 1:
        start_a(1)
    for s in range(cols):
        own_a(s).start()
    for p in order:
        own_b(p).start()
    codes_a[pl.ds(c * slots, slots), :] = code_a_ref[...]
    codes_b[pl.ds(r * slots, slots), :] = code_b_ref[...]
    for ref in buf_a + buf_b:
        ref[0] = jnp.zeros((bs, bs), ref.dtype)

    def inverse(codes, cap, keys, first_row):
        count = codes.shape[0]
        number = lax.broadcasted_iota(jnp.int32, (count, 128), 0)
        ident = (number // slots) * cap + number % cap + 1
        lane = lax.broadcasted_iota(jnp.int32, (count, 128), 1)
        for part in range(keys // 128):
            hit = codes[...] == lane + part * 128
            inv_v[pl.ds(first_row + part, 1), :] = jnp.max(
                jnp.where(hit, ident, 0), axis=0, keepdims=True)

    keys_a, keys_b = band_rows * nb, nb * band_cols
    rows_a = keys_a // 128

    def panel_traffic(p):
        for d in range(1, chips):
            @pl.when(z - d >= 0)
            def _():
                along(p, z - d, True, False).wait_recv()

                @pl.when(z < chips - 1)
                def _():
                    along(p, z - d, True, False).start()

                across(p, z - d, False).start()

            @pl.when(z + d < chips)
            def _():
                along(p, z + d, False, False).wait_recv()

                @pl.when(z > 0)
                def _():
                    along(p, z + d, False, False).start()

                across(p, z + d, False).start()

    for k, p in enumerate(order):
        s = p % cols
        if k + AHEAD < panels:
            start_own_b(order[k + AHEAD])
        if k % ratio == 0 and s + 2 < cols:
            start_a(s + 2)
        if k == 0:
            for off in range(1, cols):
                code_a(off, (c - off + cols) % cols).wait_recv()
            for off in range(1, rows):
                code_b(off, (r - off + rows) % rows).wait_recv()
            inverse(codes_a, cap_a, keys_a, 0)
            inverse(codes_b, cap_b, keys_b, rows_a)
            move = pltpu.make_async_copy(inv_v, inv_s, local_sem)
            move.start()
            move.wait()
        panel_traffic(p)
        if k % ratio == 0:
            own_a(s).wait()
            for off in range(1, cols):
                take_a(s, off).wait_recv()
        own_b(p).wait()
        for chip in range(chips):
            take_across(p, chip).wait_recv()

        def spot(key, first_row):
            return inv_s[first_row + key // 128, key % 128]

        for lr in range(band_rows):
            for lk in range(band_rows):
                at = spot(lr * nb + p * band_rows + lk, 0)
                tile_a[lr * bs : (lr + 1) * bs, lk * bs : (lk + 1) * bs] = buf_a[s][at]
        for lk in range(band_rows):
            for lc in range(band_cols):
                at = spot((p * band_rows + lk) * band_cols + lc, rows_a)
                tile_b[lk * bs : (lk + 1) * bs, lc * bs : (lc + 1) * bs] = buf_b[p][at]

        def columns(n, carry):
            where = pl.ds(pl.multiple_of(n * 256, 256), 256)
            part = jnp.dot(tile_a[...], tile_b[:, where], preferred_element_type=jnp.float32)
            if k == 0:
                o_ref[:, where] = part
            else:
                o_ref[:, where] += part
            return carry

        lax.fori_loop(0, band_cols * bs // 256, columns, 0)

    for off in range(1, cols):
        code_a(off, c).wait_send()
        for s in range(cols):
            send_a(s, off).wait_send()
    for off in range(1, rows):
        code_b(off, r).wait_send()
    for p in order:
        for chip in range(chips):
            across(p, chip, False).wait_send()

            @pl.when((z < chips - 1) & (chip <= z))
            def _():
                along(p, chip, True, False).wait_send()

            @pl.when((z > 0) & (chip >= z))
            def _():
                along(p, chip, False, False).wait_send()


def shards(a_blocks, a_coord, b_blocks, b_coord, c_mask):
    rows = lax.axis_size("row")
    cols = lax.axis_size("col")
    slots, bs = a_blocks.shape[2], a_blocks.shape[-1]
    band_rows, band_cols = c_mask.shape
    chips = rows // 2
    nb = rows * band_rows
    a_tags = a_coord.reshape(slots, 2)
    b_tags = b_coord.reshape(slots, 2)
    code_a = jnp.where(
        a_tags[:, 0] >= 0,
        (a_tags[:, 0] - lax.axis_index("row") * band_rows) * nb + a_tags[:, 1], -1)
    code_b = jnp.where(
        b_tags[:, 0] >= 0,
        b_tags[:, 0] * band_cols + b_tags[:, 1] - lax.axis_index("col") * band_cols, -1)
    code_a = jnp.broadcast_to(code_a[:, None], (slots, 128))
    code_b = jnp.broadcast_to(code_b[:, None], (slots, 128))
    inv_rows = (band_rows * nb + nb * band_cols) // 128
    inv_rows = (inv_rows + 7) // 8 * 8
    dma = pltpu.SemaphoreType.DMA
    wide, tall = band_cols * bs, band_rows * bs
    product = pl.pallas_call(
        functools.partial(kernel, rows, cols, slots, band_rows, band_cols),
        out_shape=jax.ShapeDtypeStruct((tall, wide), jnp.float32),
        in_specs=[
            pl.BlockSpec(memory_space=pl.ANY),
            pl.BlockSpec(memory_space=pl.ANY),
            pl.BlockSpec(memory_space=pltpu.VMEM),
            pl.BlockSpec(memory_space=pltpu.VMEM),
        ],
        out_specs=pl.BlockSpec(memory_space=pltpu.VMEM),
        scratch_shapes=(
            [pltpu.VMEM((1 + slots, bs, bs), jnp.bfloat16)] * cols
            + [pltpu.VMEM((1 + slots, bs, bs), jnp.bfloat16)] * rows
            + [
                pltpu.VMEM((tall, tall), jnp.bfloat16),
                pltpu.VMEM((tall, wide), jnp.bfloat16),
                pltpu.VMEM((cols * slots, 128), jnp.int32),
                pltpu.VMEM((rows * slots, 128), jnp.int32),
                pltpu.VMEM((inv_rows, 128), jnp.int32),
                pltpu.SMEM((inv_rows, 128), jnp.int32),
                dma((cols,)), dma((rows,)),
                dma((cols, cols - 1)), dma((cols, cols - 1)),
                dma((cols - 1,)), dma((cols - 1,)),
                dma((rows - 1,)), dma((rows - 1,)),
                dma((rows, chips)), dma((rows, chips)), dma((rows, chips)),
                dma((rows, chips)), dma((rows, chips)),
                dma,
            ]
        ),
        compiler_params=pltpu.CompilerParams(
            collective_id=0, has_side_effects=True, vmem_limit_bytes=52 * 2**20),
        cost_estimate=pl.CostEstimate(
            flops=2 * tall * wide * nb * bs, transcendentals=0,
            bytes_accessed=(cols + rows) * slots * bs * bs * 2 + tall * wide * 4),
    )(a_blocks.reshape(slots, bs, bs), b_blocks.reshape(slots, bs, bs), code_a, code_b)
    masked = product.reshape(band_rows, bs, band_cols, bs) * c_mask[:, None, :, None].astype(
        jnp.float32)
    return masked.reshape(tall, wide)


def solution(mesh):
    placed = (
        P("row", "col", None, None, None),
        P("row", "col", None, None),
        P("row", "col", None, None, None),
        P("row", "col", None, None),
        P("row", "col"),
    )
    return jax.shard_map(
        shards, mesh=mesh, in_specs=placed, out_specs=P("row", "col"), check_vma=False
    )
```

time: 260 us -> 106 us (0.41)
  waiting for transfers between devices: 145 us -> 0 us
  Pallas kernels: 0 us -> 97.2 us
  local copies, waits for them, and re-layouts: 40.5 us -> 2.95 us
  blocking collectives: 29.1 us -> 0 us
  starting transfers between devices: 25.8 us -> 0 us
  matrix products: 18 us -> 0 us
  other arithmetic: 0.05 us -> 4.23 us
    ppermute x14 -> x0, waiting for transfers between devices: 122 us -> none  [passed_along(): return lax.ppermute(value, axis, pairs)]
    pallas_call x0 -> x1, Pallas kernels: none -> 97.2 us  [shards(): pl.pallas_call(functools.partial(kernel, rows, cols, slots, band_rows, ba...]
    all_to_all x2 -> x0, blocking collectives: 29.1 us -> none  [the longest x1 18.8 us: shards(): lax.all_to_all(a_send, 'col', split_axis=0, concat_axis=0, tiled=True)]
    while x14 -> x0, local copies, waits for them, and re-layouts: 24.4 us -> none
    all_to_all x2 -> x0, waiting for transfers between devices: 22.3 us -> none  [the longest x1 18.4 us: shards(): lax.all_to_all(b_send, 'row', split_axis=0, concat_axis=0, tiled=True)]
    dot_general x8 -> x0, matrix products: 18 us -> none  [the longest x7 14.4 us: advance(): jnp.dot(a_use, panel_b, preferred_element_type=jnp.float32)]
    ppermute x14 -> x0, starting transfers between devices: 16.4 us -> none  [passed_along(): return lax.ppermute(value, axis, pairs)]
    all_to_all x2 -> x0, starting transfers between devices: 9.41 us -> none  [the longest x1 5.16 us: shards(): lax.all_to_all(a_tags, 'col', split_axis=0, concat_axis=0, tiled=True)]
  transfers between devices with their start and end apart: 16 -> 0, of which waited for: 9 -> 0; matrix products, arithmetic and copies ran while one was open for 12% -> 0% of each run, Pallas kernels for 0% -> 0%
where the time goes in v1:
time: 106 us; the launch traced here: 104 us
  Pallas kernels  97.2 us (92%)
  other arithmetic  4.23 us (4%)
  local copies, waits for them, and re-layouts  2.95 us (3%)
    pallas_call x1, Pallas kernels, shards(): pl.pallas_call(functools.partial(kernel, rows, cols, slots, band_rows, ba...  97.2 us
    unnamed x4, local copies, waits for them, and re-layouts  2.6 us

profile of v1, /device:TPU:0, one launch (start us, length us, event | category | flops | bytes accessed | tf_op | source)
XLA Modules:
  0.0 104.4 jit_solution(12892901268069161617)
XLA Ops:
  0.0 0.8 fusion.1
  0.8 0.8 fusion
  1.5 0.7 convert_element_type.4
  2.2 0.1 broadcast_in_dim.24.code_a_ref
  2.3 0.1 broadcast_in_dim.26.code_b_ref
  2.3 0.0 copy-start
  2.3 1.2 %copy-done = bf16[1,1,32,128,128]{4,3,2,1,0:T(8,128)(2,1)S(1)} copy-done((bf16[1,1,32,128,128]{4,3,2,1,0:T(8,128)(2,1)S(1)}, bf16[1,1,32,128,128]{4,3,2,1,0:T(8,128)(2,1)}, u32[]{:S(2)}) %copy-start) | copy-done | bytes 1048600
  3.6 97.2 %shard_map.55 = f32[512,1024]{1,0:T(8,128)} custom-call(bf16[32,128,128]{2,1,0:T(8,128)(2,1)S(1)} %bitcast.12, bf16[32,128,128]{2,1,0:T(8,128)(2,1)} %bitcast.16, s32[32,128]{1,0:T(8,128)S(1)} %broadcast_in_dim.24.code_a_ref, s32[32,128]{1,0:T(8,128)S(1)} %broadcast_in_dim.26.code_b_ref), custom_call_target="tpu_custom_call" | custom-call | flops 4294967296 | bytes 14680064 | tf_op jit(solution)/shard_map/pallas_call | solution.py:270
  100.8 0.0 copy-start.1
  100.8 0.2 mul.37
  101.0 1.4 %copy-done.1 = f32[512,1024]{1,0:T(8,128)S(1)} copy-done((f32[512,1024]{1,0:T(8,128)S(1)}, f32[512,1024]{1,0:T(8,128)}, u32[]{:S(2)}) %copy-start.1) | copy-done | bytes 2097176
  102.4 2.0 %bitcast_multiply_fusion = f32[512,1024]{1,0:T(8,128)} fusion(f32[512,1024]{1,0:T(8,128)S(1)} %copy-done.1, f32[64,8,8,128]{3,2,1,0:T(8,128)S(1)} %bitcast.13), kind=kLoop, calls=%fused_computation | loop fusion | flops 524288 | bytes 6291456 | tf_op jit(solution)/shard_map/mul | solution.py:305
Async XLA Ops:
  2.3 1.2 %copy-start = (bf16[1,1,32,128,128]{4,3,2,1,0:T(8,128)(2,1)S(1)}, bf16[1,1,32,128,128]{4,3,2,1,0:T(8,128)(2,1)}, u32[]{:S(2)}) copy-start(bf16[1,1,32,128,128]{4,3,2,1,0:T(8,128)(2,1)} %param.5) | copy-start | bytes 3145732
  100.8 1.6 %copy-start.1 = (f32[512,1024]{1,0:T(8,128)S(1)}, f32[512,1024]{1,0:T(8,128)}, u32[]{:S(2)}) copy-start(f32[512,1024]{1,0:T(8,128)} %shard_map.55) | copy-start | bytes 6291460

commit v2 on v1

--- a/solution.py
+++ b/solution.py
@@ -13,7 +13,7 @@
 
 def kernel(
     rows, cols, slots, band_rows, band_cols,
-    a_ref, b_ref, code_a_ref, code_b_ref, o_ref, *scratch,
+    a_ref, b_ref, tags_a_ref, tags_b_ref, mask_ref, o_ref, *scratch,
 ):
     panels = rows
     chips = rows // 2
@@ -24,7 +24,7 @@
     buf_a = scratch[:cols]
     buf_b = scratch[cols : cols + panels]
     (
-        tile_a, tile_b, codes_a, codes_b, inv_v, inv_s,
+        tile_a, tile_b, code_a_ref, code_b_ref, codes_a, codes_b, inv_v, inv_s,
         own_a_sem, own_b_sem, a_send, a_recv, ca_send, ca_recv, cb_send, cb_recv,
         up_send, down_send, z_recv, sib_send, sib_recv, local_sem,
     ) = scratch[cols + panels :]
@@ -99,13 +99,13 @@
 
     def code_a(off, source):
         return pltpu.make_async_remote_copy(
-            src_ref=code_a_ref, dst_ref=codes_a.at[pl.ds(source * slots, slots)],
+            src_ref=code_a_ref, dst_ref=codes_a.at[pl.ds(source * 8, 8)],
             send_sem=ca_send.at[off - 1], recv_sem=ca_recv.at[off - 1],
             device_id=(r, (c + off) % cols), device_id_type=MESH)
 
     def code_b(off, source):
         return pltpu.make_async_remote_copy(
-            src_ref=code_b_ref, dst_ref=codes_b.at[pl.ds(source * slots, slots)],
+            src_ref=code_b_ref, dst_ref=codes_b.at[pl.ds(source * 8, 8)],
             send_sem=cb_send.at[off - 1], recv_sem=cb_recv.at[off - 1],
             device_id=((r + off) % rows, c), device_id_type=MESH)
 
@@ -124,6 +124,13 @@
         for off in range(1, cols):
             send_a(s, off).start()
 
+    def note(tags, code_ref, across_part, down_part):
+        code = jnp.where(tags[0:1, :] >= 0, across_part(tags[0:1, :]) + down_part(tags[1:2, :]), -1)
+        code_ref[...] = jnp.full((8, 128), -1, jnp.int32)
+        code_ref[:, :slots] = jnp.broadcast_to(code, (8, slots))
+
+    note(tags_a_ref, code_a_ref, lambda x: (x - r * band_rows) * nb, lambda x: x)
+    note(tags_b_ref, code_b_ref, lambda x: x * band_cols, lambda x: x - c * band_cols)
     pl.semaphore_wait(barrier, rows + cols - 2)
     start_own_b(order[0])
     start_a(0)
@@ -139,52 +146,55 @@
         own_a(s).start()
     for p in order:
         own_b(p).start()
-    codes_a[pl.ds(c * slots, slots), :] = code_a_ref[...]
-    codes_b[pl.ds(r * slots, slots), :] = code_b_ref[...]
+    codes_a[pl.ds(pl.multiple_of(c * 8, 8), 8), :] = code_a_ref[...]
+    codes_b[pl.ds(pl.multiple_of(r * 8, 8), 8), :] = code_b_ref[...]
     for ref in buf_a + buf_b:
         ref[0] = jnp.zeros((bs, bs), ref.dtype)
 
     def inverse(codes, cap, keys, first_row):
-        count = codes.shape[0]
-        number = lax.broadcasted_iota(jnp.int32, (count, 128), 0)
-        ident = (number // slots) * cap + number % cap + 1
-        lane = lax.broadcasted_iota(jnp.int32, (count, 128), 1)
+        number = lax.broadcasted_iota(jnp.int32, (slots, 128), 0)
+        lane = lax.broadcasted_iota(jnp.int32, (slots, 128), 1)
+        found = [jnp.zeros((slots, 128), jnp.int32) for _ in range(keys // 128)]
+        for source in range(codes.shape[0] // 8):
+            row = codes[source * 8 : source * 8 + 1, :]
+            column = jnp.broadcast_to(row, (128, 128)).T[:slots, :]
+            ident = source * cap + number % cap + 1
+            for part in range(keys // 128):
+                found[part] = jnp.where(column == lane + part * 128, ident, found[part])
         for part in range(keys // 128):
-            hit = codes[...] == lane + part * 128
-            inv_v[pl.ds(first_row + part, 1), :] = jnp.max(
-                jnp.where(hit, ident, 0), axis=0, keepdims=True)
+            inv_v[first_row + part : first_row + part + 1, :] = jnp.max(
+                found[part], axis=0, keepdims=True)
 
     keys_a, keys_b = band_rows * nb, nb * band_cols
     rows_a = keys_a // 128
 
-    def panel_traffic(p):
-        for d in range(1, chips):
-            @pl.when(z - d >= 0)
+    def hop(p, d):
+        @pl.when(z - d >= 0)
+        def _():
+            along(p, z - d, True, False).wait_recv()
+
+            @pl.when(z < chips - 1)
             def _():
-                along(p, z - d, True, False).wait_recv()
-
-                @pl.when(z < chips - 1)
-                def _():
-                    along(p, z - d, True, False).start()
-
-                across(p, z - d, False).start()
-
-            @pl.when(z + d < chips)
+                along(p, z - d, True, False).start()
+
+            across(p, z - d, False).start()
+
+        @pl.when(z + d < chips)
+        def _():
+            along(p, z + d, False, False).wait_recv()
+
+            @pl.when(z > 0)
             def _():
-                along(p, z + d, False, False).wait_recv()
-
-                @pl.when(z > 0)
-                def _():
-                    along(p, z + d, False, False).start()
-
-                across(p, z + d, False).start()
-
-    for k, p in enumerate(order):
+                along(p, z + d, False, False).start()
+
+            across(p, z + d, False).start()
+
+    def spot(key, first_row):
+        return inv_s[first_row + key // 128, key % 128]
+
+    def gather_a(k):
+        p = order[k]
         s = p % cols
-        if k + AHEAD < panels:
-            start_own_b(order[k + AHEAD])
-        if k % ratio == 0 and s + 2 < cols:
-            start_a(s + 2)
         if k == 0:
             for off in range(1, cols):
                 code_a(off, (c - off + cols) % cols).wait_recv()
@@ -195,37 +205,58 @@
             move = pltpu.make_async_copy(inv_v, inv_s, local_sem)
             move.start()
             move.wait()
-        panel_traffic(p)
         if k % ratio == 0:
             own_a(s).wait()
             for off in range(1, cols):
                 take_a(s, off).wait_recv()
-        own_b(p).wait()
-        for chip in range(chips):
-            take_across(p, chip).wait_recv()
-
-        def spot(key, first_row):
-            return inv_s[first_row + key // 128, key % 128]
-
         for lr in range(band_rows):
             for lk in range(band_rows):
                 at = spot(lr * nb + p * band_rows + lk, 0)
                 tile_a[lr * bs : (lr + 1) * bs, lk * bs : (lk + 1) * bs] = buf_a[s][at]
+        own_b(p).wait()
+        for chip in range(chips):
+            take_across(p, chip).wait_recv()
+
+    pair = 2 * bs
+
+    def columns(k, n):
+        p = order[k]
         for lk in range(band_rows):
-            for lc in range(band_cols):
-                at = spot((p * band_rows + lk) * band_cols + lc, rows_a)
-                tile_b[lk * bs : (lk + 1) * bs, lc * bs : (lc + 1) * bs] = buf_b[p][at]
-
-        def columns(n, carry):
-            where = pl.ds(pl.multiple_of(n * 256, 256), 256)
-            part = jnp.dot(tile_a[...], tile_b[:, where], preferred_element_type=jnp.float32)
-            if k == 0:
-                o_ref[:, where] = part
-            else:
-                o_ref[:, where] += part
-            return carry
-
-        lax.fori_loop(0, band_cols * bs // 256, columns, 0)
+            for half in range(2):
+                at = spot((p * band_rows + lk) * band_cols + n * 2 + half, rows_a)
+                tile_b[lk * bs : (lk + 1) * bs, half * bs : (half + 1) * bs] = buf_b[p][at]
+        part = jnp.dot(tile_a[...], tile_b[...], preferred_element_type=jnp.float32)
+        where = slice(n * pair, (n + 1) * pair)
+        if k > 0:
+            part = o_ref[:, where] + part
+        if k < panels - 1:
+            o_ref[:, where] = part
+        else:
+            for lr in range(band_rows):
+                for half in range(2):
+                    lc = n * 2 + half
+                    o_ref[lr * bs : (lr + 1) * bs, lc * bs : (lc + 1) * bs] = part[
+                        lr * bs : (lr + 1) * bs, half * bs : (half + 1) * bs
+                    ] * mask_ref[lr, lc].astype(jnp.float32)
+
+    def work(k):
+        parts = [functools.partial(gather_a, k)]
+        return parts + [functools.partial(columns, k, n) for n in range(band_cols // 2)]
+
+    for k, p in enumerate(order):
+        s = p % cols
+        if k + AHEAD < panels:
+            start_own_b(order[k + AHEAD])
+        if k % ratio == 0 and s + 2 < cols:
+            start_a(s + 2)
+        parts = work(k - 1) if k > 0 else []
+        share = -(-len(parts) // (chips - 1))
+        for d in range(1, chips):
+            hop(p, d)
+            for part in parts[(d - 1) * share : d * share]:
+                part()
+    for part in work(panels - 1):
+        part()
 
     for off in range(1, cols):
         code_a(off, c).wait_send()
@@ -253,21 +284,13 @@
     band_rows, band_cols = c_mask.shape
     chips = rows // 2
     nb = rows * band_rows
-    a_tags = a_coord.reshape(slots, 2)
-    b_tags = b_coord.reshape(slots, 2)
-    code_a = jnp.where(
-        a_tags[:, 0] >= 0,
-        (a_tags[:, 0] - lax.axis_index("row") * band_rows) * nb + a_tags[:, 1], -1)
-    code_b = jnp.where(
-        b_tags[:, 0] >= 0,
-        b_tags[:, 0] * band_cols + b_tags[:, 1] - lax.axis_index("col") * band_cols, -1)
-    code_a = jnp.broadcast_to(code_a[:, None], (slots, 128))
-    code_b = jnp.broadcast_to(code_b[:, None], (slots, 128))
+    a_tags = a_coord.reshape(slots, 2).T
+    b_tags = b_coord.reshape(slots, 2).T
     inv_rows = (band_rows * nb + nb * band_cols) // 128
     inv_rows = (inv_rows + 7) // 8 * 8
     dma = pltpu.SemaphoreType.DMA
     wide, tall = band_cols * bs, band_rows * bs
-    product = pl.pallas_call(
+    return pl.pallas_call(
         functools.partial(kernel, rows, cols, slots, band_rows, band_cols),
         out_shape=jax.ShapeDtypeStruct((tall, wide), jnp.float32),
         in_specs=[
@@ -275,6 +298,7 @@
             pl.BlockSpec(memory_space=pl.ANY),
             pl.BlockSpec(memory_space=pltpu.VMEM),
             pl.BlockSpec(memory_space=pltpu.VMEM),
+            pl.BlockSpec(memory_space=pltpu.SMEM),
         ],
         out_specs=pl.BlockSpec(memory_space=pltpu.VMEM),
         scratch_shapes=(
@@ -282,9 +306,11 @@
             + [pltpu.VMEM((1 + slots, bs, bs), jnp.bfloat16)] * rows
             + [
                 pltpu.VMEM((tall, tall), jnp.bfloat16),
-                pltpu.VMEM((tall, wide), jnp.bfloat16),
-                pltpu.VMEM((cols * slots, 128), jnp.int32),
-                pltpu.VMEM((rows * slots, 128), jnp.int32),
+                pltpu.VMEM((tall, 2 * bs), jnp.bfloat16),
+                pltpu.VMEM((8, 128), jnp.int32),
+                pltpu.VMEM((8, 128), jnp.int32),
+                pltpu.VMEM((cols * 8, 128), jnp.int32),
+                pltpu.VMEM((rows * 8, 128), jnp.int32),
                 pltpu.VMEM((inv_rows, 128), jnp.int32),
                 pltpu.SMEM((inv_rows, 128), jnp.int32),
                 dma((cols,)), dma((rows,)),
@@ -297,14 +323,11 @@
             ]
         ),
         compiler_params=pltpu.CompilerParams(
-            collective_id=0, has_side_effects=True, vmem_limit_bytes=52 * 2**20),
+            collective_id=0, has_side_effects=True, vmem_limit_bytes=62 * 2**20),
         cost_estimate=pl.CostEstimate(
             flops=2 * tall * wide * nb * bs, transcendentals=0,
             bytes_accessed=(cols + rows) * slots * bs * bs * 2 + tall * wide * 4),
-    )(a_blocks.reshape(slots, bs, bs), b_blocks.reshape(slots, bs, bs), code_a, code_b)
-    masked = product.reshape(band_rows, bs, band_cols, bs) * c_mask[:, None, :, None].astype(
-        jnp.float32)
-    return masked.reshape(tall, wide)
+    )(a_blocks.reshape(slots, bs, bs), b_blocks.reshape(slots, bs, bs), a_tags, b_tags, c_mask)
 
 
 def solution(mesh):

time: 106 us -> 84.9 us (0.80)
  Pallas kernels: 97.2 us -> 81 us
  other arithmetic: 4.23 us -> 0 us
    pallas_call x1, Pallas kernels: 97.2 us -> 81 us  [shards(): pl.pallas_call(functools.partial(kernel, rows, cols, slots, band_rows, ba...]
    mul x1 -> x0, other arithmetic: 2.03 us -> none  [shards(): product.reshape(band_rows, bs, band_cols, bs)]
    broadcast_in_dim x2 -> x0, other arithmetic: 1.52 us -> none  [the longest x1 0.76 us: shards(): code_b = jnp.broadcast_to(code_b[:, None], (slots, 128))]
    unnamed x4 -> x1, local copies, waits for them, and re-layouts: 2.6 us -> 3.16 us
where the time goes in v2:
time: 84.9 us; the launch traced here: 84.2 us
  Pallas kernels  81 us (95%)
  local copies, waits for them, and re-layouts  3.16 us (4%)
    pallas_call x1, Pallas kernels, shards(): pl.pallas_call(functools.partial(kernel, rows, cols, slots, band_rows, ba...  81 us
    unnamed x1, local copies, waits for them, and re-layouts  3.16 us

profile of v2, /device:TPU:0, one launch (start us, length us, event | category | flops | bytes accessed | tf_op | source)
XLA Modules:
  0.0 84.2 jit_solution(9453630551088821230)
XLA Ops:
  0.0 81.0 %shard_map.55 = f32[512,1024]{1,0:T(8,128)} custom-call(bf16[32,128,128]{2,1,0:T(8,128)(2,1)} %bitcast.8, bf16[32,128,128]{2,1,0:T(8,128)(2,1)} %bitcast.9, s32[2,32]{1,0:T(2,128)} %bitcast.10, s32[2,32]{1,0:T(2,128)} %bitcast.11, s32[4,8]{1,0:T(4,128)} %mask_ref.1), custom_call_target="tpu_custom_call" | custom-call | flops 4294967296 | bytes 14680064 | tf_op jit(solution)/shard_map/pallas_call | solution.py:293
  81.0 3.2 %copy.7 = f32[512,1024]{1,0:T(8,128)} copy(f32[512,1024]{1,0:T(8,128)} %shard_map.55) | data formatting | bytes 4194304

commit v3 on v2

--- a/solution.py
+++ b/solution.py
@@ -13,7 +13,7 @@
 
 def kernel(
     rows, cols, slots, band_rows, band_cols,
-    a_ref, b_ref, tags_a_ref, tags_b_ref, mask_ref, o_ref, *scratch,
+    a_ref, b_ref, tags_a_ref, tags_b_ref, mask_ref, out_ref, *scratch,
 ):
     panels = rows
     chips = rows // 2
@@ -24,7 +24,7 @@
     buf_a = scratch[:cols]
     buf_b = scratch[cols : cols + panels]
     (
-        tile_a, tile_b, code_a_ref, code_b_ref, codes_a, codes_b, inv_v, inv_s,
+        o_ref, out_sem, tiles_a, tile_b, code_a_ref, code_b_ref, codes_a, codes_b, inv_v, inv_s,
         own_a_sem, own_b_sem, a_send, a_recv, ca_send, ca_recv, cb_send, cb_recv,
         up_send, down_send, z_recv, sib_send, sib_recv, local_sem,
     ) = scratch[cols + panels :]
@@ -212,12 +212,19 @@
         for lr in range(band_rows):
             for lk in range(band_rows):
                 at = spot(lr * nb + p * band_rows + lk, 0)
-                tile_a[lr * bs : (lr + 1) * bs, lk * bs : (lk + 1) * bs] = buf_a[s][at]
+                tiles_a[k % 2, lr * bs : (lr + 1) * bs, lk * bs : (lk + 1) * bs] = buf_a[s][at]
+
+    def settle_b(k):
+        p = order[k]
         own_b(p).wait()
         for chip in range(chips):
             take_across(p, chip).wait_recv()
 
     pair = 2 * bs
+
+    def leave(n):
+        where = pl.ds(n * pair, pair)
+        return pltpu.make_async_copy(o_ref.at[:, where], out_ref.at[:, where], out_sem.at[n])
 
     def columns(k, n):
         p = order[k]
@@ -225,7 +232,7 @@
             for half in range(2):
                 at = spot((p * band_rows + lk) * band_cols + n * 2 + half, rows_a)
                 tile_b[lk * bs : (lk + 1) * bs, half * bs : (half + 1) * bs] = buf_b[p][at]
-        part = jnp.dot(tile_a[...], tile_b[...], preferred_element_type=jnp.float32)
+        part = jnp.dot(tiles_a[k % 2], tile_b[...], preferred_element_type=jnp.float32)
         where = slice(n * pair, (n + 1) * pair)
         if k > 0:
             part = o_ref[:, where] + part
@@ -238,9 +245,12 @@
                     o_ref[lr * bs : (lr + 1) * bs, lc * bs : (lc + 1) * bs] = part[
                         lr * bs : (lr + 1) * bs, half * bs : (half + 1) * bs
                     ] * mask_ref[lr, lc].astype(jnp.float32)
+            leave(n).start()
 
     def work(k):
-        parts = [functools.partial(gather_a, k)]
+        parts = [functools.partial(settle_b, k)]
+        if k < panels - 1:
+            parts = [functools.partial(gather_a, k)] + parts
         return parts + [functools.partial(columns, k, n) for n in range(band_cols // 2)]
 
     for k, p in enumerate(order):
@@ -255,9 +265,13 @@
             hop(p, d)
             for part in parts[(d - 1) * share : d * share]:
                 part()
+            if k == panels - 1 and d == max(chips - 2, 1):
+                gather_a(k)
     for part in work(panels - 1):
         part()
 
+    for n in range(band_cols // 2):
+        leave(n).wait()
     for off in range(1, cols):
         code_a(off, c).wait_send()
         for s in range(cols):
@@ -300,12 +314,14 @@
             pl.BlockSpec(memory_space=pltpu.VMEM),
             pl.BlockSpec(memory_space=pltpu.SMEM),
         ],
-        out_specs=pl.BlockSpec(memory_space=pltpu.VMEM),
+        out_specs=pl.BlockSpec(memory_space=pl.ANY),
         scratch_shapes=(
             [pltpu.VMEM((1 + slots, bs, bs), jnp.bfloat16)] * cols
             + [pltpu.VMEM((1 + slots, bs, bs), jnp.bfloat16)] * rows
             + [
-                pltpu.VMEM((tall, tall), jnp.bfloat16),
+                pltpu.VMEM((tall, wide), jnp.float32),
+                dma((band_cols // 2,)),
+                pltpu.VMEM((2, tall, tall), jnp.bfloat16),
                 pltpu.VMEM((tall, 2 * bs), jnp.bfloat16),
                 pltpu.VMEM((8, 128), jnp.int32),
                 pltpu.VMEM((8, 128), jnp.int32),

time: 84.9 us -> 84.7 us (level)
  no operation moved by 1% of the time
where the time goes in v3:
time: 84.7 us; the launch traced here: 84.1 us
  Pallas kernels  81 us (96%)
  local copies, waits for them, and re-layouts  3.16 us (4%)
    pallas_call x1, Pallas kernels, shards(): pl.pallas_call(functools.partial(kernel, rows, cols, slots, band_rows, ba...  81 us
    unnamed x1, local copies, waits for them, and re-layouts  3.16 us

profile of v3, /device:TPU:0, one launch (start us, length us, event | category | flops | bytes accessed | tf_op | source)
XLA Modules:
  0.0 84.1 jit_solution(18146189263904131574)
XLA Ops:
  0.0 81.0 %shard_map.55 = f32[512,1024]{1,0:T(8,128)} custom-call(bf16[32,128,128]{2,1,0:T(8,128)(2,1)} %bitcast.8, bf16[32,128,128]{2,1,0:T(8,128)(2,1)} %bitcast.9, s32[2,32]{1,0:T(2,128)} %bitcast.10, s32[2,32]{1,0:T(2,128)} %bitcast.11, s32[4,8]{1,0:T(4,128)} %mask_ref.1), custom_call_target="tpu_custom_call" | custom-call | flops 4294967296 | bytes 14680064 | tf_op jit(solution)/shard_map/pallas_call | solution.py:307
  81.0 3.2 %copy.7 = f32[512,1024]{1,0:T(8,128)} copy(f32[512,1024]{1,0:T(8,128)} %shard_map.55) | data formatting | bytes 4194304
